TPU v7x, 32 devices: a whole 2x2x4 slice. The times are simulated.
32 devices in a mesh: replica: 4 (over z), fsdp: 4 (over y, x), ctx: 2 (over core).
Axes of the slice: x: 2, y: 2, z: 4, core: 2. Of those that a mesh axis runs over, the one named last changes fastest.
Arguments:
- tokens: bfloat16 [32, 1024, 1024], P(('replica', 'fsdp'), 'ctx'), may hold values from -6 to 6
- segments: int32 [32, 1024], P(('replica', 'fsdp')), may hold values from 0 to 2, as said below
- attn_gain: bfloat16 [1024], P(('fsdp', 'ctx')), may hold values from 0.25 to 1.75
- query_weight: bfloat16 [1024, 1024], P(('fsdp', 'ctx')), may hold values from -0.1875 to 0.1875
- key_weight: bfloat16 [1024, 512], P(('fsdp', 'ctx')), may hold values from -0.1875 to 0.1875
- value_weight: bfloat16 [1024, 512], P(('fsdp', 'ctx')), may hold values from -0.1875 to 0.1875
- output_weight: bfloat16 [1024, 1024], P(('fsdp', 'ctx')), may hold values from -0.75 to 0.75
- query_gain: bfloat16 [64], P(('fsdp', 'ctx')), may hold values from 0.25 to 1.75
- key_gain: bfloat16 [64], P(('fsdp', 'ctx')), may hold values from 0.25 to 1.75
- ffn_gain: bfloat16 [1024], P(('fsdp', 'ctx')), may hold values from 0.25 to 1.75
- gate_weight: bfloat16 [1024, 4608], P(('fsdp', 'ctx')), may hold values from -0.1875 to 0.1875
- up_weight: bfloat16 [1024, 4608], P(('fsdp', 'ctx')), may hold values from -0.1875 to 0.1875
- down_weight: bfloat16 [4608, 1024], P(('fsdp', 'ctx')), may hold values from -0.09375 to 0.09375
- cotangent: bfloat16 [32, 1024, 1024], P(('replica', 'fsdp'), 'ctx'), may hold values from -6 to 6
Outputs:
- output: bfloat16 [32, 1024, 1024], P(('replica', 'fsdp'), 'ctx')
- input_grad: float32 [32, 1024, 1024], P(('replica', 'fsdp'), 'ctx')
- grad_attn_gain: float32 [1024], P(('fsdp', 'ctx'))
- grad_w_query: float32 [1024, 1024], P(('fsdp', 'ctx'))
- grad_w_key: float32 [1024, 512], P(('fsdp', 'ctx'))
- grad_w_value: float32 [1024, 512], P(('fsdp', 'ctx'))
- grad_w_out: float32 [1024, 1024], P(('fsdp', 'ctx'))
- grad_query_gain: float32 [64], P(('fsdp', 'ctx'))
- grad_key_gain: float32 [64], P(('fsdp', 'ctx'))
- grad_ffn_gain: float32 [1024], P(('fsdp', 'ctx'))
- grad_w_gate: float32 [1024, 4608], P(('fsdp', 'ctx'))
- grad_w_up: float32 [1024, 4608], P(('fsdp', 'ctx'))
- grad_w_down: float32 [4608, 1024], P(('fsdp', 'ctx'))
Inputs may be any that keep to these rules, and one draw needn't show every extreme that they name: `segments`: never falls along a sequence; every sequence holds documents 0, 1 and 2, each of one token or more, and document 1 holds positions 256 to 767.
All inputs are finite; a program needn't handle non-finite values.
Results may differ from a plain program's by a relative error of at most 0.028.
Values may be sent and summed in bfloat16 or wider, within the bound.
A program may use at most 256 MiB of HBM per device.

v0:
```python
import jax
import jax.numpy as jnp
from jax import lax
from jax.sharding import PartitionSpec as P

epsilon = 1e-05
rope_base = 1000000.0
neg_fill = -1e30


def rms_scale(values):
    return lax.rsqrt(jnp.mean(values * values, axis=-1, keepdims=True) + epsilon)


def rotate(values, cosine, sine):
    half_dim = values.shape[-1] // 2
    turned = jnp.concatenate([-values[..., half_dim:], values[..., :half_dim]], axis=-1)
    return values * cosine + turned * sine


def rotate_back(values, cosine, sine):
    scaled = values * sine
    half_dim = values.shape[-1] // 2
    turned = jnp.concatenate([scaled[..., half_dim:], -scaled[..., :half_dim]], axis=-1)
    return values * cosine + turned


def norm_back(grad_in, normed, factor):
    return factor * (grad_in - normed * jnp.mean(grad_in * normed, axis=-1, keepdims=True))


def rounded(values):
    return lax.optimization_barrier(values.astype(jnp.bfloat16)).astype(jnp.float32)


def gather_attention(
    attn_gain, query_weight, key_weight, value_weight, output_weight, query_gain, key_gain
):
    return (
        lax.all_gather(attn_gain, ("fsdp", "ctx"), axis=0, tiled=True),
        lax.all_gather(query_weight, ("fsdp", "ctx"), axis=0, tiled=True),
        lax.all_gather(key_weight, ("fsdp", "ctx"), axis=0, tiled=True),
        lax.all_gather(value_weight, ("fsdp", "ctx"), axis=0, tiled=True),
        lax.all_gather(output_weight, ("fsdp", "ctx"), axis=0, tiled=True),
        lax.all_gather(query_gain, ("fsdp", "ctx"), axis=0, tiled=True),
        lax.all_gather(key_gain, ("fsdp", "ctx"), axis=0, tiled=True),
    )


def gather_feed(ffn_gain, gate_weight, up_weight, down_weight):
    return (
        lax.all_gather(ffn_gain, ("fsdp", "ctx"), axis=0, tiled=True),
        lax.all_gather(gate_weight, ("fsdp", "ctx"), axis=0, tiled=True),
        lax.all_gather(up_weight, ("fsdp", "ctx"), axis=0, tiled=True),
        lax.all_gather(down_weight, ("fsdp", "ctx"), axis=0, tiled=True),
    )


def gather_keys(key_local, value_local):
    return (
        lax.all_gather(key_local, "ctx", axis=1, tiled=True),
        lax.all_gather(value_local, "ctx", axis=1, tiled=True),
    )


def split_keys(whole, kv_count, head_dim):
    seq_count, seq_len, kv_width = whole.shape
    return whole.reshape(seq_count, seq_len, kv_count, head_dim).transpose(2, 0, 1, 3)


def per_device(
    tokens,
    segments,
    attn_gain,
    query_weight,
    key_weight,
    value_weight,
    output_weight,
    query_gain,
    key_gain,
    ffn_gain,
    gate_weight,
    up_weight,
    down_weight,
    cotangent,
):
    seq_count, span_len, width = tokens.shape
    seq_len = segments.shape[1]
    tok_count = seq_count * span_len
    attn_set = gather_attention(
        attn_gain, query_weight, key_weight, value_weight, output_weight, query_gain, key_gain
    )
    feed_set = gather_feed(ffn_gain, gate_weight, up_weight, down_weight)
    gain_one = attn_set[0].astype(jnp.float32)
    gain_query = attn_set[5].astype(jnp.float32)
    gain_key = attn_set[6].astype(jnp.float32)
    gain_two = feed_set[0].astype(jnp.float32)
    head_dim = gain_query.shape[0]
    head_count = attn_set[1].shape[1] // head_dim
    kv_count = attn_set[2].shape[1] // head_dim
    kv_width = kv_count * head_dim
    group_size = head_count // kv_count
    score_scale = head_dim ** (-0.5)
    first_pos = lax.axis_index("ctx") * span_len
    input_rows = tokens.astype(jnp.float32).reshape(tok_count, width)
    factor_one = rms_scale(input_rows)
    normed_one = input_rows * factor_one
    hidden_input = (normed_one * gain_one).astype(jnp.bfloat16)
    query_unrotated = jnp.dot(hidden_input, attn_set[1], preferred_element_type=jnp.float32)
    key_unrotated = jnp.dot(hidden_input, attn_set[2], preferred_element_type=jnp.float32)
    value_low = jnp.dot(hidden_input, attn_set[3], preferred_element_type=jnp.float32).astype(
        jnp.bfloat16
    )
    query_heads = query_unrotated.reshape(tok_count, head_count, head_dim)
    query_factor = rms_scale(query_heads)
    query_normed = query_heads * query_factor
    key_heads = key_unrotated.reshape(tok_count, kv_count, head_dim)
    key_factor = rms_scale(key_heads)
    key_normed = key_heads * key_factor
    own_segs = lax.dynamic_slice_in_dim(segments, first_pos, span_len, 1)
    query_index = first_pos + jnp.arange(span_len, dtype=jnp.int32)
    key_index = jnp.arange(seq_len, dtype=jnp.int32)
    same_doc = own_segs[:, :, None] == segments[:, None, :]
    positions = jnp.sum(
        (same_doc & (key_index[None, None, :] < query_index[None, :, None])).astype(jnp.int32),
        axis=-1,
    )
    allowed = (same_doc & (key_index[None, None, :] <= query_index[None, :, None]))[:, None]
    freq = jnp.power(
        jnp.float32(rope_base), -jnp.arange(head_dim // 2, dtype=jnp.float32) * 2.0 / head_dim
    )
    angle = positions.astype(jnp.float32).reshape(tok_count, 1, 1) * freq
    angle = jnp.concatenate([angle, angle], axis=-1)
    cosine = jnp.cos(angle)
    sine = jnp.sin(angle)
    query_low = rotate(query_normed * gain_query, cosine, sine).astype(jnp.bfloat16)
    key_low = rotate(key_normed * gain_key, cosine, sine).astype(jnp.bfloat16)
    key_send = key_low.reshape(seq_count, span_len, kv_width)
    value_send = value_low.reshape(seq_count, span_len, kv_width)
    key_whole, value_whole = gather_keys(key_send, value_send)
    query_t = query_low.reshape(seq_count, span_len, kv_count, group_size, head_dim).transpose(
        2, 0, 3, 1, 4
    )
    key_t = split_keys(key_whole, kv_count, head_dim)
    value_t = split_keys(value_whole, kv_count, head_dim)

    def attend(bundle):
        query_blk, key_blk, value_blk = bundle
        scores = (
            jnp.einsum("sgqd,skd->sgqk", query_blk, key_blk, preferred_element_type=jnp.float32)
            * score_scale
        )
        masked = jnp.where(allowed, scores, neg_fill)
        row_max = jnp.max(masked, axis=-1, keepdims=True)
        expo = jnp.exp(masked - row_max)
        row_sum = jnp.sum(expo, axis=-1, keepdims=True)
        probs = (expo / row_sum).astype(jnp.bfloat16)
        mixed_blk = jnp.einsum(
            "sgqk,skd->sgqd", probs, value_blk, preferred_element_type=jnp.float32
        )
        return (mixed_blk, row_max[..., 0] + jnp.log(row_sum[..., 0]))

    mixed_t, log_sums = lax.map(attend, (query_t, key_t, value_t))
    mixed_low = (
        mixed_t.transpose(1, 3, 0, 2, 4)
        .reshape(tok_count, head_count * head_dim)
        .astype(jnp.bfloat16)
    )
    residual_stream = input_rows + jnp.dot(
        mixed_low, attn_set[4], preferred_element_type=jnp.float32
    )
    factor_two = rms_scale(residual_stream)
    normed_two = residual_stream * factor_two
    hidden_second = (normed_two * gain_two).astype(jnp.bfloat16)
    gate_rows = jnp.dot(hidden_second, feed_set[1], preferred_element_type=jnp.float32)
    up_projected = jnp.dot(hidden_second, feed_set[2], preferred_element_type=jnp.float32)
    sigma = jax.nn.sigmoid(gate_rows)
    silu_gate = gate_rows * sigma
    act_low = (silu_gate * up_projected).astype(jnp.bfloat16)
    result = residual_stream + jnp.dot(act_low, feed_set[3], preferred_element_type=jnp.float32)
    output = result.astype(jnp.bfloat16).reshape(seq_count, span_len, width)
    feed_set = gather_feed(ffn_gain, gate_weight, up_weight, down_weight)
    attn_set = gather_attention(
        attn_gain, query_weight, key_weight, value_weight, output_weight, query_gain, key_gain
    )
    key_whole, value_whole = gather_keys(key_send, value_send)
    key_t = split_keys(key_whole, kv_count, head_dim)
    value_t = split_keys(value_whole, kv_count, head_dim)
    grad_out = cotangent.astype(jnp.float32).reshape(tok_count, width)
    grad_out_low = grad_out.astype(jnp.bfloat16)
    grad_down = jnp.einsum("rf,rd->fd", act_low, grad_out_low, preferred_element_type=jnp.float32)
    grad_act = jnp.einsum(
        "rd,fd->rf", grad_out_low, feed_set[3], preferred_element_type=jnp.float32
    )
    grad_gate = (grad_act * up_projected * (sigma * (1.0 + gate_rows * (1.0 - sigma)))).astype(
        jnp.bfloat16
    )
    grad_up = (grad_act * silu_gate).astype(jnp.bfloat16)
    grad_gate_w = jnp.einsum(
        "rd,rf->df", hidden_second, grad_gate, preferred_element_type=jnp.float32
    )
    grad_up_w = jnp.einsum("rd,rf->df", hidden_second, grad_up, preferred_element_type=jnp.float32)
    grad_two = jnp.einsum("rf,df->rd", grad_gate, feed_set[1], preferred_element_type=jnp.float32)
    grad_two = grad_two + jnp.einsum(
        "rf,df->rd", grad_up, feed_set[2], preferred_element_type=jnp.float32
    )
    grad_gain_two = jnp.sum(grad_two * normed_two, axis=0)
    feed_grads = (
        lax.psum_scatter(grad_gain_two, ("fsdp", "ctx"), scatter_dimension=0, tiled=True),
        lax.psum_scatter(grad_gate_w, ("fsdp", "ctx"), scatter_dimension=0, tiled=True),
        lax.psum_scatter(grad_up_w, ("fsdp", "ctx"), scatter_dimension=0, tiled=True),
        lax.psum_scatter(grad_down, ("fsdp", "ctx"), scatter_dimension=0, tiled=True),
    )
    grad_resid = grad_out + norm_back(grad_two * gain_two, normed_two, factor_two)
    grad_branch = grad_resid.astype(jnp.bfloat16)
    grad_out_w = jnp.einsum("re,rd->ed", mixed_low, grad_branch, preferred_element_type=jnp.float32)
    grad_mixed = jnp.einsum(
        "rd,ed->re", grad_branch, attn_set[4], preferred_element_type=jnp.float32
    ).astype(jnp.bfloat16)
    grad_mixed_t = grad_mixed.reshape(
        seq_count, span_len, kv_count, group_size, head_dim
    ).transpose(2, 0, 3, 1, 4)

    def attend_back(bundle):
        query_blk, key_blk, value_blk, grad_blk, lse_blk = bundle
        scores = (
            jnp.einsum("sgqd,skd->sgqk", query_blk, key_blk, preferred_element_type=jnp.float32)
            * score_scale
        )
        masked = jnp.where(allowed, scores, neg_fill)
        probs = jnp.exp(masked - lse_blk[..., None])
        probs_low = probs.astype(jnp.bfloat16)
        grad_value_blk = jnp.einsum(
            "sgqk,sgqd->skd", probs_low, grad_blk, preferred_element_type=jnp.float32
        )
        grad_probs = jnp.einsum(
            "sgqd,skd->sgqk", grad_blk, value_blk, preferred_element_type=jnp.float32
        )
        grad_scores = (
            probs * (grad_probs - jnp.sum(probs * grad_probs, axis=-1, keepdims=True))
        ).astype(jnp.bfloat16)
        grad_query_blk = (
            jnp.einsum("sgqk,skd->sgqd", grad_scores, key_blk, preferred_element_type=jnp.float32)
            * score_scale
        )
        grad_key_blk = (
            jnp.einsum("sgqk,sgqd->skd", grad_scores, query_blk, preferred_element_type=jnp.float32)
            * score_scale
        )
        return (grad_query_blk, grad_key_blk, grad_value_blk)

    grad_query_t, grad_key_t, grad_value_t = lax.map(
        attend_back, (query_t, key_t, value_t, grad_mixed_t, log_sums)
    )
    grad_key_all = grad_key_t.transpose(1, 2, 0, 3).reshape(seq_count, seq_len, kv_width)
    grad_value_all = grad_value_t.transpose(1, 2, 0, 3).reshape(seq_count, seq_len, kv_width)
    grad_key_own, grad_value_own = (
        lax.psum_scatter(
            grad_key_all.astype(jnp.bfloat16), "ctx", scatter_dimension=1, tiled=True
        ).astype(jnp.float32),
        lax.psum_scatter(
            grad_value_all.astype(jnp.bfloat16), "ctx", scatter_dimension=1, tiled=True
        ).astype(jnp.float32),
    )
    grad_value_low = grad_value_own.astype(jnp.bfloat16).reshape(tok_count, kv_width)
    grad_key_rot = rounded(grad_key_own).reshape(tok_count, kv_count, head_dim)
    grad_query_rot = rounded(grad_query_t.transpose(1, 3, 0, 2, 4)).reshape(
        tok_count, head_count, head_dim
    )
    grad_query_normed = rotate_back(grad_query_rot, cosine, sine)
    grad_gain_query = jnp.sum(grad_query_normed * query_normed, axis=(0, 1))
    grad_query_pre = norm_back(grad_query_normed * gain_query, query_normed, query_factor)
    grad_query_pre = grad_query_pre.reshape(tok_count, head_count * head_dim).astype(jnp.bfloat16)
    grad_key_normed = rotate_back(grad_key_rot, cosine, sine)
    grad_gain_key = jnp.sum(grad_key_normed * key_normed, axis=(0, 1))
    grad_key_pre = norm_back(grad_key_normed * gain_key, key_normed, key_factor)
    grad_key_pre = grad_key_pre.reshape(tok_count, kv_width).astype(jnp.bfloat16)
    grad_query_w = jnp.einsum(
        "rd,re->de", hidden_input, grad_query_pre, preferred_element_type=jnp.float32
    )
    grad_key_w = jnp.einsum(
        "rd,re->de", hidden_input, grad_key_pre, preferred_element_type=jnp.float32
    )
    grad_value_w = jnp.einsum(
        "rd,re->de", hidden_input, grad_value_low, preferred_element_type=jnp.float32
    )
    grad_one = jnp.einsum(
        "re,de->rd", grad_query_pre, attn_set[1], preferred_element_type=jnp.float32
    )
    grad_one = grad_one + jnp.einsum(
        "re,de->rd", grad_key_pre, attn_set[2], preferred_element_type=jnp.float32
    )
    grad_one = grad_one + jnp.einsum(
        "re,de->rd", grad_value_low, attn_set[3], preferred_element_type=jnp.float32
    )
    grad_gain_one = jnp.sum(grad_one * normed_one, axis=0)
    input_grad = grad_resid + norm_back(grad_one * gain_one, normed_one, factor_one)
    attn_grads = (
        lax.psum_scatter(grad_gain_one, ("fsdp", "ctx"), scatter_dimension=0, tiled=True),
        lax.psum_scatter(grad_query_w, ("fsdp", "ctx"), scatter_dimension=0, tiled=True),
        lax.psum_scatter(grad_key_w, ("fsdp", "ctx"), scatter_dimension=0, tiled=True),
        lax.psum_scatter(grad_value_w, ("fsdp", "ctx"), scatter_dimension=0, tiled=True),
        lax.psum_scatter(grad_out_w, ("fsdp", "ctx"), scatter_dimension=0, tiled=True),
        lax.psum_scatter(grad_gain_query, ("fsdp", "ctx"), scatter_dimension=0, tiled=True),
        lax.psum_scatter(grad_gain_key, ("fsdp", "ctx"), scatter_dimension=0, tiled=True),
    )
    totals = (
        lax.psum(attn_grads[0].astype(jnp.bfloat16), "replica").astype(jnp.float32),
        lax.psum(attn_grads[1].astype(jnp.bfloat16), "replica").astype(jnp.float32),
        lax.psum(attn_grads[2].astype(jnp.bfloat16), "replica").astype(jnp.float32),
        lax.psum(attn_grads[3].astype(jnp.bfloat16), "replica").astype(jnp.float32),
        lax.psum(attn_grads[4].astype(jnp.bfloat16), "replica").astype(jnp.float32),
        lax.psum(attn_grads[5].astype(jnp.bfloat16), "replica").astype(jnp.float32),
        lax.psum(attn_grads[6].astype(jnp.bfloat16), "replica").astype(jnp.float32),
        lax.psum(feed_grads[0].astype(jnp.bfloat16), "replica").astype(jnp.float32),
        lax.psum(feed_grads[1].astype(jnp.bfloat16), "replica").astype(jnp.float32),
        lax.psum(feed_grads[2].astype(jnp.bfloat16), "replica").astype(jnp.float32),
        lax.psum(feed_grads[3].astype(jnp.bfloat16), "replica").astype(jnp.float32),
    )
    return (
        output,
        input_grad.reshape(seq_count, span_len, width),
        totals[0],
        totals[1],
        totals[2],
        totals[3],
        totals[4],
        totals[5],
        totals[6],
        totals[7],
        totals[8],
        totals[9],
        totals[10],
    )


def solution(mesh):
    in_specs = (
        P(("replica", "fsdp"), "ctx", None),
        P(("replica", "fsdp"), None),
        P(("fsdp", "ctx")),
        P(("fsdp", "ctx"), None),
        P(("fsdp", "ctx"), None),
        P(("fsdp", "ctx"), None),
        P(("fsdp", "ctx"), None),
        P(("fsdp", "ctx")),
        P(("fsdp", "ctx")),
        P(("fsdp", "ctx")),
        P(("fsdp", "ctx"), None),
        P(("fsdp", "ctx"), None),
        P(("fsdp", "ctx"), None),
        P(("replica", "fsdp"), "ctx", None),
    )
    out_specs = (
        P(("replica", "fsdp"), "ctx", None),
        P(("replica", "fsdp"), "ctx", None),
        P(("fsdp", "ctx")),
        P(("fsdp", "ctx"), None),
        P(("fsdp", "ctx"), None),
        P(("fsdp", "ctx"), None),
        P(("fsdp", "ctx"), None),
        P(("fsdp", "ctx")),
        P(("fsdp", "ctx")),
        P(("fsdp", "ctx")),
        P(("fsdp", "ctx"), None),
        P(("fsdp", "ctx"), None),
        P(("fsdp", "ctx"), None),
    )
    return jax.shard_map(
        per_device, mesh=mesh, in_specs=in_specs, out_specs=out_specs, check_vma=False
    )
```

profile of v0, /device:TPU:0, one launch (start us, length us, event | category | flops | bytes accessed | tf_op | source)
XLA Modules:
  0.0 1360.7 jit_solution(10012892274923072035)
XLA Ops:
  23.5 13.2 all-reduce.7
  79.9 11.6 all-gather.12.cloned.1.call-done
  121.9 88.8 %while.28 = (s32[]{:T(128)}, bf16[8,2,2,512,64]{3,4,2,1,0:T(8,128)(2,1)}, f32[8,2,2,512]{3,2,1,0:T(2,128)}, bf16[8,2,2,512,64]{3,4,2,1,0:T(8,128)(2,1)}, bf16[8,...) while((s32[]{:T(128)}, ...), condition=%wide.region_7.8_spmd.clone, body=%wide.region_4.7_spmd.clone.sunk | while | flops 564131840 | bytes 31275620 | solution.py:163
  224.5 17.7 %fusion.80 = f32[1024,4608]{1,0:T(8,128)} fusion(bf16[1024,1024]{1,0:T(8,128)(2,1)S(1)} %multiply_convert_fusion.5, bf16[1024,4608]{1,0:T(8,128)(2,1)} %all-gather.24.cloned.1.call-done), kind=kOutput, calls=%fused_computation.150 | convolution fusion | flops 9663676416 | bytes 30408704 | tf_op jit(solution)/shard_map/dot_general | solution.py:175
  242.2 27.3 %all-gather.26.cloned.1.call-done = bf16[1024,4608]{1,0:T(8,128)(2,1)} async-done(((bf16[128,4608]{1,0:T(8,128)(2,1)}), bf16[1024,4608]{1,0:T(8,128)(2,1)}) %all-gather.26.cloned.1.call-update) | async-done | bytes 9437200 | tf_op jit(solution)/shard_map/all_gather | solution.py:54
  269.6 16.5 %fusion.81 = f32[1024,4608]{1,0:T(8,128)} fusion(bf16[1024,1024]{1,0:T(8,128)(2,1)S(1)} %multiply_convert_fusion.5, bf16[1024,4608]{1,0:T(8,128)(2,1)} %all-gather.26.cloned.1.call-done), kind=kOutput, calls=%fused_computation.151 | convolution fusion | flops 9663676416 | bytes 30408704 | tf_op jit(solution)/shard_map/dot_general | solution.py:176
  286.0 44.3 %all-gather.28.cloned.1.call-done = bf16[4608,1024]{1,0:T(8,128)(2,1)} async-done(((bf16[576,1024]{1,0:T(8,128)(2,1)}), bf16[4608,1024]{1,0:T(8,128)(2,1)}) %all-gather.28.cloned.1.call-update) | async-done | bytes 9437200 | tf_op jit(solution)/shard_map/all_gather | solution.py:55
  330.3 31.5 %multiply_convert_fusion.1 = (bf16[1024,4608]{1,0:T(8,128)(2,1)}, bf16[1024,4608]{1,0:T(8,128)(2,1)}, bf16[1024,4608]{1,0:T(8,128)(2,1)}) fusion(f32[1024,4608]{1,0:T(8,128)} %fusion.80, f32[1024,4608]{1,0:T(8,128)} %fusion.81, bf16[1024,1024]{1,0:T(8,128)(2,1)} %bitcast.277, bf16[4608,1024]{1,0:T(8,128)(2,1)} %all-gather.28.cloned.1.call-done), kind=kOutput, calls=%fused_computation.60 | convolution fusion | flops 9734455296 | bytes 77594624 | tf_op jit(solution)/shard_map/rd,fd->rf/dot_general | solution.py:192
  361.9 16.0 %fusion.82 = f32[1024,1024]{1,0:T(8,128)} fusion(bf16[1024,4608]{1,0:T(8,128)(2,1)} %get-tuple-element.320, bf16[1024,4608]{1,0:T(8,128)(2,1)} %all-gather.24.cloned.1.call-done), kind=kOutput, calls=%fused_computation.152 | convolution fusion | flops 9663676416 | bytes 23068672 | tf_op jit(solution)/shard_map/rf,df->rd/dot_general | solution.py:203
  377.9 17.4 %multiply_reduce_fusion.1 = (f32[1024]{0:T(1024)}, f32[1024]{0:T(1024)S(1)}, f32[1024,1024]{1,0:T(8,128)S(1)}) fusion(f32[1024,1024]{1,0:T(8,128)S(1)} %copy-done.10, f32[1024]{0:T(1024)S(1)} %add_rsqrt_fusion.2, f32[1024]{0:T(1024)S(1)} %bitcast.292, f32[1024,1024]{1,0:T(8,128)} %fusion.82, bf16[1024,4608]{1,0:T(8,128)(2,1)} %get-tuple-element.319, ...), kind=kOutput, calls=%fused_computation.86 | convolution fusion | flops 9671014400 | bytes 31473664 | tf_op jit(solution)/shard_map/rf,df->rd/dot_general | solution.py:204
  408.5 157.2 %while.29 = (s32[]{:T(128)}, bf16[8,2,2,512,64]{3,4,2,1,0:T(8,128)(2,1)S(1)}, bf16[8,2,1024,64]{2,3,0,1:T(8,128)(2,1)}, bf16[8,2,1024,64]{2,3,0,1:T(8,128)(2,1)}...) while((s32[]{:T(128)}, ...), condition=%wide.region_12.13_spmd.clone, body=%wide.region_10.12_spmd.clone.sunk | while | flops 1375991808 | bytes 71639168 | solution.py:252
  618.9 17.0 %fusion.87 = f32[1024,4608]{1,0:T(8,128)} fusion(bf16[1024,1024]{1,0:T(8,128)(2,1)} %copy-done.21, bf16[1024,4608]{1,0:T(8,128)(2,1)} %get-tuple-element.320), kind=kOutput, calls=%fused_computation.157 | convolution fusion | flops 9663676416 | bytes 30408704 | tf_op jit(solution)/shard_map/rd,rf->df/dot_general | solution.py:199
  637.5 16.5 %fusion.88 = f32[1024,4608]{1,0:T(8,128)} fusion(bf16[1024,1024]{1,0:T(8,128)(2,1)S(1)} %copy-done.22, bf16[1024,4608]{1,0:T(8,128)(2,1)} %get-tuple-element.319), kind=kOutput, calls=%fused_computation.158 | convolution fusion | flops 9663676416 | bytes 30408704 | tf_op jit(solution)/shard_map/rd,rf->df/dot_general | solution.py:202
  655.6 16.9 %fusion.89 = f32[4608,1024]{1,0:T(8,128)} fusion(bf16[1024,4608]{1,0:T(8,128)(2,1)} %get-tuple-element.321, bf16[1024,1024]{1,0:T(8,128)(2,1)S(1)} %bitcast.278), kind=kOutput, calls=%fused_computation.159 | convolution fusion | flops 9663676416 | bytes 30408704 | tf_op jit(solution)/shard_map/rf,rd->fd/dot_general | solution.py:191
  675.9 23.5 %reduce-scatter.14.cloned.1.call-done = f32[128,1024]{1,0:T(8,128)} async-done(((f32[1024,1024]{1,0:T(8,128)}), f32[128,1024]{1,0:T(8,128)}) %reduce-scatter.14.cloned.1.call-update) | async-done | bytes 524304 | tf_op jit(solution)/shard_map/reduce_scatter | solution.py:300
  701.2 43.2 %reduce-scatter.16.cloned.1.call-done = f32[128,512]{1,0:T(8,128)} async-done(((f32[1024,512]{1,0:T(8,128)}), f32[128,512]{1,0:T(8,128)}) %reduce-scatter.16.cloned.1.call-update) | async-done | bytes 262160 | tf_op jit(solution)/shard_map/reduce_scatter | solution.py:301
  746.0 43.7 %reduce-scatter.18.cloned.1.call-done = f32[128,512]{1,0:T(8,128)} async-done(((f32[1024,512]{1,0:T(8,128)}), f32[128,512]{1,0:T(8,128)}) %reduce-scatter.18.cloned.1.call-update) | async-done | bytes 262160 | tf_op jit(solution)/shard_map/reduce_scatter | solution.py:302
  791.3 128.0 %reduce-scatter.22.cloned.1.call-done = f32[128,4608]{1,0:T(8,128)} async-done(((f32[1024,4608]{1,0:T(8,128)}), f32[128,4608]{1,0:T(8,128)}) %reduce-scatter.22.cloned.1.call-update) | async-done | bytes 2359312 | tf_op jit(solution)/shard_map/reduce_scatter | solution.py:210
  922.1 126.8 %reduce-scatter.24.cloned.1.call-done = f32[128,4608]{1,0:T(8,128)} async-done(((f32[1024,4608]{1,0:T(8,128)}), f32[128,4608]{1,0:T(8,128)}) %reduce-scatter.24.cloned.1.call-update) | async-done | bytes 2359312 | tf_op jit(solution)/shard_map/reduce_scatter | solution.py:211
  1051.7 126.8 %reduce-scatter.26.cloned.1.call-done = f32[576,1024]{1,0:T(8,128)} async-done(((f32[4608,1024]{1,0:T(8,128)}), f32[576,1024]{1,0:T(8,128)}) %reduce-scatter.26.cloned.1.call-update) | async-done | bytes 2359312 | tf_op jit(solution)/shard_map/reduce_scatter | solution.py:212
  1187.5 16.5 %add_convert_fusion = bf16[1024,1024]{1,0:T(8,128)(2,1)} fusion(f32[1024,1024]{1,0:T(8,128)S(1)} %copy-done.11, bf16[1024,4608]{1,0:T(8,128)(2,1)} %get-tuple-element.321, bf16[4608,1024]{1,0:T(8,128)(2,1)} %all-gather.28.cloned.1.call-done), kind=kOutput, calls=%fused_computation.93 | convolution fusion | flops 9665773568 | bytes 25165824 | tf_op jit(solution)/shard_map/dot_general | solution.py:180
  1211.9 24.9 %all-reduce.6 = (bf16[1024]{0:T(1024)(128)(2,1)S(1)}, bf16[64]{0:T(256)(128)(2,1)S(1)}, bf16[64]{0:T(256)(128)(2,1)S(1)}, bf16[1024]{0:T(1024)(128)(2,1)S(1)}) all-reduce(f32[1024]{0:T(1024)S(1)} %get-tuple-element.250, f32[64]{0:T(128)S(1)} %get-tuple-element.246, ...), channel_id=4, replica_groups=mesh['replica'=4,'fsdp'=4,'ctx'=2] {'fsdp','ctx'}, use_global_device_ids=true, to_apply=%region_19.20.clone | all-reduce | flops 2176 | bytes 13056
  1237.1 12.3 all-reduce.8
  1256.9 87.3 %all-reduce.12.cloned.1.call-done = (bf16[128,1024]{1,0:T(8,128)(2,1)}, bf16[128,512]{1,0:T(8,128)(2,1)}, bf16[128,512]{1,0:T(8,128)(2,1)}, bf16[128,1024]{1,0:T...) async-done(((bf16[128,1024]{1,0:T(8,128)(2,1)}, bf16[128,512]{1,0:T(8,128)(2,1)}, bf16[128,512]{1,0:T(8,128)(2,1)}, ...) | async-done | bytes 4325392 | tf_op jit(solution)/shard_map/psum | solution.py:309
  (373 shorter events, 463.9 us)
Async XLA Ops:
  7.2 36.0 %all-gather.14.cloned.1.call-start = ((), (), s32[]{:S(2)}) async-start(), calls=%async_computation.10 | async-start | bytes 1179648 | tf_op jit(solution)/shard_map/all_gather | solution.py:42
  7.9 53.7 %all-gather.18.cloned.1.call-start = ((), (), s32[]{:S(2)}) async-start(), calls=%async_computation.12 | async-start | bytes 1179648 | tf_op jit(solution)/shard_map/all_gather | solution.py:43
  8.7 82.8 %all-gather.12.cloned.1.call-start = ((), (), s32[]{:S(2)}) async-start(), calls=%async_computation.9 | async-start | bytes 2359296 | tf_op jit(solution)/shard_map/all_gather | solution.py:41
  9.4 103.3 %all-gather.16.cloned.1.call-start = ((), (), s32[]{:S(2)}) async-start(), calls=%async_computation.11 | async-start | bytes 3145728 | tf_op jit(solution)/shard_map/all_gather | solution.py:61
  19.8 37.1 %copy-start.43 = (f32[8,1,128]{2,1,0:T(1,128)}, f32[8,1,128]{2,1,0:T(1,128)S(1)}, u32[]{:S(2)}) copy-start(f32[8,1,128]{2,1,0:T(1,128)S(1)} %convert_element_type.258) | copy-start | bytes 12292
  40.8 60.4 %copy-start.13 = (f32[1024,64]{0,1:T(8,128)}, f32[1024,64]{0,1:T(8,128)S(1)}, u32[]{:S(2)}) copy-start(f32[1024,64]{0,1:T(8,128)S(1)} %get-tuple-element.330) | copy-start | bytes 786436
  40.8 60.4 %copy-start.15 = (f32[1024,64]{0,1:T(8,128)}, f32[1024,64]{0,1:T(8,128)S(1)}, u32[]{:S(2)}) copy-start(f32[1024,64]{0,1:T(8,128)S(1)} %get-tuple-element.331) | copy-start | bytes 786436
  56.8 60.4 %all-gather.20.cloned.1.call-start = ((), (), s32[]{:S(2)}) async-start(), calls=%async_computation.13 | async-start | bytes 3145728 | tf_op jit(solution)/shard_map/all_gather | solution.py:62
  68.0 148.5 %all-gather.22.cloned.1.call-start = ((), (), s32[]{:S(2)}) async-start(), calls=%async_computation.14 | async-start | bytes 2359296 | tf_op jit(solution)/shard_map/all_gather | solution.py:44
  68.6 155.9 %all-gather.24.cloned.1.call-start = ((), (), s32[]{:S(2)}) async-start(), calls=%async_computation.15 | async-start | bytes 10616832 | tf_op jit(solution)/shard_map/all_gather | solution.py:53
  69.4 200.2 %all-gather.26.cloned.1.call-start = ((), (), s32[]{:S(2)}) async-start(), calls=%async_computation.16 | async-start | bytes 10616832 | tf_op jit(solution)/shard_map/all_gather | solution.py:54
  70.1 260.2 %all-gather.28.cloned.1.call-start = ((), (), s32[]{:S(2)}) async-start(), calls=%async_computation.17 | async-start | bytes 10616832 | tf_op jit(solution)/shard_map/all_gather | solution.py:55
  70.8 529.6 %reduce-scatter.10.cloned.1.call-start = ((), (), s32[]{:S(2)}) async-start(), calls=%async_computation.18 | async-start | bytes 3145728 | tf_op jit(solution)/shard_map/reduce_scatter | solution.py:258
  224.5 45.1 %copy-start.21 = (bf16[1024,1024]{1,0:T(8,128)(2,1)}, bf16[1024,1024]{1,0:T(8,128)(2,1)S(1)}, u32[]{:S(2)}) copy-start(bf16[1024,1024]{1,0:T(8,128)(2,1)S(1)} %multiply_convert_fusion.5) | copy-start | bytes 6291460
  565.6 49.0 %reduce-scatter.12.cloned.1.call-start = ((), (), s32[]{:S(2)}) async-start(), calls=%async_computation.19 | async-start | bytes 3145728 | tf_op jit(solution)/shard_map/reduce_scatter | solution.py:261
  566.4 107.8 %reduce-scatter.20.cloned.1.call-start = ((), (), s32[]{:S(2)}) async-start(), calls=%async_computation.23 | async-start | bytes 4718592 | tf_op jit(solution)/shard_map/reduce_scatter | solution.py:303
  573.6 125.8 %reduce-scatter.14.cloned.1.call-start = ((), (), s32[]{:S(2)}) async-start(), calls=%async_computation.20 | async-start | bytes 4718592 | tf_op jit(solution)/shard_map/reduce_scatter | solution.py:300
  600.4 144.0 %reduce-scatter.16.cloned.1.call-start = ((), (), s32[]{:S(2)}) async-start(), calls=%async_computation.21 | async-start | bytes 2359296 | tf_op jit(solution)/shard_map/reduce_scatter | solution.py:301
  614.6 175.1 %reduce-scatter.18.cloned.1.call-start = ((), (), s32[]{:S(2)}) async-start(), calls=%async_computation.22 | async-start | bytes 2359296 | tf_op jit(solution)/shard_map/reduce_scatter | solution.py:302
  618.9 300.4 %reduce-scatter.22.cloned.1.call-start = ((), (), s32[]{:S(2)}) async-start(), calls=%async_computation.24 | async-start | bytes 21233664 | tf_op jit(solution)/shard_map/reduce_scatter | solution.py:210
  635.9 413.0 %reduce-scatter.24.cloned.1.call-start = ((), (), s32[]{:S(2)}) async-start(), calls=%async_computation.25 | async-start | bytes 21233664 | tf_op jit(solution)/shard_map/reduce_scatter | solution.py:211
  654.0 524.6 %reduce-scatter.26.cloned.1.call-start = ((), (), s32[]{:S(2)}) async-start(), calls=%async_computation.26 | async-start | bytes 21233664 | tf_op jit(solution)/shard_map/reduce_scatter | solution.py:212
  672.5 671.7 %all-reduce.12.cloned.1.call-start = ((), (), s32[]{:S(2)}) async-start(), calls=%async_computation.27 | async-start | bytes 8650752 | tf_op jit(solution)/shard_map/psum | solution.py:309
  1051.7 129.7 %copy-start.18 = (bf16[1024,1024]{1,0:T(8,128)(2,1)S(1)}, bf16[1024,1024]{1,0:T(8,128)(2,1)}, u32[]{:S(2)}) copy-start(bf16[1024,1024]{1,0:T(8,128)(2,1)} %all-gather.12.cloned.1.call-done) | copy-start | bytes 6291460
  (49 other events, 265.1 us)
Sparse Core Ops, SparseCore 0:
  9.9 26.2 all-gather.13
  38.1 23.4 all-gather.17
  63.5 27.8 all-gather.11
  93.4 10.5 all-gather.15
  105.4 11.7 all-gather.19
  119.0 29.0 all-gather.21
  150.0 58.8 all-gather.23
  210.7 58.8 all-gather.25
  271.5 58.8 all-gather.27
  565.8 9.5 reduce-scatter.9
  577.7 10.7 reduce-scatter.11
  591.8 52.5 reduce-scatter.19
  648.0 51.3 reduce-scatter.13
  703.1 41.1 reduce-scatter.15
  748.4 41.2 reduce-scatter.17
  793.1 126.1 reduce-scatter.21
  922.8 126.1 reduce-scatter.23
  1052.4 126.1 reduce-scatter.25
  1182.6 161.5 all-reduce.11
where the time goes:
time: 1370 us; the launch traced here: 1360 us
  waiting for transfers between devices  672 us (49%)
  matrix products  392 us (29%)
  other arithmetic  113 us (8%)
  local copies, waits for them, and re-layouts  95.1 us (7%)
  blocking collectives  69.6 us (5%)
  between operations  17.2 us (1%)
    reduce_scatter x1, waiting for transfers between devices, per_device(): lax.psum_scatter(grad_gate_w, ('fsdp', 'ctx'), scatter_dimension=0, tiled...  128 us
    reduce_scatter x1, waiting for transfers between devices, per_device(): lax.psum_scatter(grad_down, ('fsdp', 'ctx'), scatter_dimension=0, tiled=T...  127 us
    reduce_scatter x1, waiting for transfers between devices, per_device(): lax.psum_scatter(grad_up_w, ('fsdp', 'ctx'), scatter_dimension=0, tiled=T...  127 us
    psum x1, waiting for transfers between devices, per_device(): lax.psum(attn_grads[1].astype(jnp.bfloat16), 'replica').astype(jnp.float32)  87.3 us
    all_gather x1, waiting for transfers between devices, gather_feed(): lax.all_gather(down_weight, ('fsdp', 'ctx'), axis=0, tiled=True)  44.3 us
    reduce_scatter x1, waiting for transfers between devices, per_device(): lax.psum_scatter(grad_value_w, ('fsdp', 'ctx'), scatter_dimension=0, tile...  43.7 us
    reduce_scatter x1, waiting for transfers between devices, per_device(): lax.psum_scatter(grad_key_w, ('fsdp', 'ctx'), scatter_dimension=0, tiled=...  43.2 us
    unnamed x2, blocking collectives  38.1 us
  transfers between devices with their start and end apart: 19, of which 12 were waited for; matrix products, arithmetic and copies ran while one was open for 25% of the time, Pallas kernels for 0%

commit v1 on v0

v1 whole, which is shorter than its diff:
```python
import jax
import jax.numpy as jnp
from jax import lax
from jax.experimental import pallas as pl
from jax.experimental.pallas import tpu as pltpu
from jax.sharding import PartitionSpec as P

epsilon = 1e-05
rope_base = 1000000.0
log2_e = 1.4426950408889634
row_block = 256
f32 = jnp.float32
bf16 = jnp.bfloat16


def rms_scale(values):
    return lax.rsqrt(jnp.mean(values * values, axis=-1, keepdims=True) + epsilon)


def norm_back(grad_in, normed, factor):
    return factor * (grad_in - normed * jnp.mean(grad_in * normed, axis=-1, keepdims=True))


def dot_nt(left, right):
    return lax.dot_general(left, right, (((1,), (1,)), ((), ())), preferred_element_type=f32)


def dot_tn(left, right):
    return lax.dot_general(left, right, (((0,), (0,)), ((), ())), preferred_element_type=f32)


def dot_nn(left, right):
    return jnp.dot(left, right, preferred_element_type=f32)


def block_mask(seg_col, seg_row, first, count):
    same = seg_col == seg_row
    row_at = first + lax.broadcasted_iota(jnp.int32, same.shape, 0)
    key_at = lax.broadcasted_iota(jnp.int32, same.shape, 1)
    return same & (key_at <= row_at)


def attend_kernel(head_dim, group, kv_per, query, key, value, seg_col, seg_row, mixed, logs):
    seq_len = query.shape[0]
    size = min(row_block, seq_len)
    factor = log2_e * head_dim**-0.5
    for first in range(0, seq_len, size):
        last = first + size
        mask = block_mask(
            seg_col[0, first:last, :], seg_row[0, :, :last], first, size
        )
        pieces = []
        log_cols = []
        for kv in range(kv_per):
            key_blk = key[:last, kv * head_dim : (kv + 1) * head_dim]
            value_blk = value[:last, kv * head_dim : (kv + 1) * head_dim]
            for member in range(group):
                at = (kv * group + member) * head_dim
                scores = dot_nt(query[first:last, at : at + head_dim], key_blk)
                expo = jnp.where(mask, jnp.exp2(scores * factor), 0.0)
                total = jnp.sum(expo, axis=-1, keepdims=True)
                out = dot_nn(expo.astype(bf16), value_blk)
                pieces.append((out / total).astype(bf16))
                log_cols.append(jnp.log2(total))
        mixed[first:last, :] = jnp.concatenate(pieces, axis=1)
        logs[0, first:last, :] = jnp.concatenate(log_cols, axis=1)


def attend_back_kernel(
    head_dim,
    group,
    kv_per,
    query,
    key,
    value,
    seg_col,
    seg_row,
    mixed,
    grad_mixed,
    logs,
    grad_query,
    grad_key,
    grad_value,
    key_sum,
    value_sum,
):
    seq_len = query.shape[0]
    size = min(row_block, seq_len)
    scale = head_dim**-0.5
    factor = log2_e * scale
    key_sum[...] = jnp.zeros_like(key_sum)
    value_sum[...] = jnp.zeros_like(value_sum)
    for first in range(0, seq_len, size):
        last = first + size
        mask = block_mask(
            seg_col[0, first:last, :], seg_row[0, :, :last], first, size
        )
        pieces = []
        for kv in range(kv_per):
            key_blk = key[:last, kv * head_dim : (kv + 1) * head_dim]
            value_blk = value[:last, kv * head_dim : (kv + 1) * head_dim]
            for member in range(group):
                head = kv * group + member
                at = head * head_dim
                query_blk = query[first:last, at : at + head_dim]
                grad_blk = grad_mixed[first:last, at : at + head_dim]
                mixed_blk = mixed[first:last, at : at + head_dim]
                delta = jnp.sum(
                    grad_blk.astype(f32) * mixed_blk.astype(f32), axis=-1, keepdims=True
                )
                scores = dot_nt(query_blk, key_blk)
                log_col = logs[0, first:last, head : head + 1]
                probs = jnp.where(mask, jnp.exp2(scores * factor - log_col), 0.0)
                grad_probs = dot_nt(grad_blk, value_blk)
                grad_scores = (probs * (grad_probs - delta)).astype(bf16)
                value_sum[kv, :last, :] += dot_tn(probs.astype(bf16), grad_blk)
                key_sum[kv, :last, :] += dot_tn(grad_scores, query_blk)
                pieces.append((dot_nn(grad_scores, key_blk) * scale).astype(bf16))
        grad_query[first:last, :] = jnp.concatenate(pieces, axis=1)
    grad_key[...] = jnp.concatenate(
        [(key_sum[kv] * scale).astype(bf16) for kv in range(kv_per)], axis=1
    )
    grad_value[...] = jnp.concatenate(
        [value_sum[kv].astype(bf16) for kv in range(kv_per)], axis=1
    )


def attend_specs(seq_len, head_dim, group, kv_per):
    wide = pl.BlockSpec((seq_len, kv_per * group * head_dim), lambda s, h: (s, h))
    narrow = pl.BlockSpec((seq_len, kv_per * head_dim), lambda s, h: (s, h))
    seg_col = pl.BlockSpec((1, seq_len, 1), lambda s, h: (s, 0, 0))
    seg_row = pl.BlockSpec((1, 1, seq_len), lambda s, h: (s, 0, 0))
    return wide, narrow, seg_col, seg_row


def attend(query, key, value, segments, head_dim, group):
    seq_count, seq_len = segments.shape
    kv_count = key.shape[1] // head_dim
    kv_per = 2 if kv_count % 2 == 0 else kv_count
    steps = kv_count // kv_per
    wide, narrow, seg_col, seg_row = attend_specs(seq_len, head_dim, group, kv_per)
    logs = pl.BlockSpec((1, seq_len, kv_per * group), lambda s, h: (s * steps + h, 0, 0))
    heads = kv_count * group
    work = seq_count * heads * seq_len * seq_len

    def body(*refs):
        attend_kernel(head_dim, group, kv_per, *refs)

    return pl.pallas_call(
        body,
        grid=(seq_count, steps),
        in_specs=[wide, narrow, narrow, seg_col, seg_row],
        out_specs=[wide, logs],
        out_shape=[
            jax.ShapeDtypeStruct(query.shape, bf16),
            jax.ShapeDtypeStruct((seq_count * steps, seq_len, kv_per * group), f32),
        ],
        compiler_params=pltpu.CompilerParams(vmem_limit_bytes=40 * 1024 * 1024),
        cost_estimate=pl.CostEstimate(
            flops=4 * work * head_dim, bytes_accessed=8 * query.size, transcendentals=work
        ),
    )(query, key, value, segments[:, :, None], segments[:, None, :])


def attend_back(query, key, value, segments, mixed, grad_mixed, logs, head_dim, group):
    seq_count, seq_len = segments.shape
    kv_count = key.shape[1] // head_dim
    kv_per = logs.shape[2] // group
    steps = kv_count // kv_per
    wide, narrow, seg_col, seg_row = attend_specs(seq_len, head_dim, group, kv_per)
    log_spec = pl.BlockSpec((1, seq_len, kv_per * group), lambda s, h: (s * steps + h, 0, 0))
    heads = kv_count * group
    work = seq_count * heads * seq_len * seq_len

    def body(*refs):
        attend_back_kernel(head_dim, group, kv_per, *refs)

    return pl.pallas_call(
        body,
        grid=(seq_count, steps),
        in_specs=[wide, narrow, narrow, seg_col, seg_row, wide, wide, log_spec],
        out_specs=[wide, narrow, narrow],
        out_shape=[
            jax.ShapeDtypeStruct(query.shape, bf16),
            jax.ShapeDtypeStruct(key.shape, bf16),
            jax.ShapeDtypeStruct(key.shape, bf16),
        ],
        scratch_shapes=[
            pltpu.VMEM((kv_per, seq_len, head_dim), f32),
            pltpu.VMEM((kv_per, seq_len, head_dim), f32),
        ],
        compiler_params=pltpu.CompilerParams(vmem_limit_bytes=40 * 1024 * 1024),
        cost_estimate=pl.CostEstimate(
            flops=10 * work * head_dim, bytes_accessed=16 * query.size, transcendentals=work
        ),
    )(query, key, value, segments[:, :, None], segments[:, None, :], mixed, grad_mixed, logs)


def make_per_device():
    swap = [(0, 1), (1, 0)]

    def partner(values):
        return lax.ppermute(values, "ctx", swap)

    def in_order(side, own, other, axis):
        first = jnp.where(side == 0, own, other)
        second = jnp.where(side == 0, other, own)
        return jnp.concatenate([first, second], axis=axis)

    def pick(side, values, axis):
        return lax.dynamic_index_in_dim(values, side, axis, keepdims=False)

    def halves(side, weight, block):
        rows = weight.shape[0]
        cut = weight.reshape(rows, -1, 2, block)
        zero = cut[:, :, 0, :].reshape(rows, -1)
        one = cut[:, :, 1, :].reshape(rows, -1)
        return jnp.where(side == 0, zero, one), jnp.where(side == 0, one, zero)

    def gather_columns(side, weights, blocks):
        own, other = zip(*(halves(side, w, b) for w, b in zip(weights, blocks)))
        own = jnp.concatenate(own, axis=1)
        other = jnp.concatenate(other, axis=1)
        shard = in_order(side, own, partner(other), 0)
        return lax.all_gather(shard, "fsdp", axis=0, tiled=True)

    def scatter_rows(grad):
        return lax.psum_scatter(grad, "fsdp", scatter_dimension=0, tiled=True)

    def total_after(shard, earlier):
        shard, earlier = lax.optimization_barrier((shard, earlier))
        return lax.psum(shard, "replica"), earlier

    def restore_columns(side, shard, widths, blocks):
        cut = shard.reshape(2, -1, shard.shape[1])
        own = pick(side, cut, 0)
        other = partner(pick(1 - side, cut, 0))
        outs = []
        at = 0
        for width, block in zip(widths, blocks):
            mine = own[:, at : at + width].reshape(own.shape[0], -1, 1, block)
            theirs = other[:, at : at + width].reshape(own.shape[0], -1, 1, block)
            outs.append(in_order(side, mine, theirs, 2).reshape(own.shape[0], 2 * width).astype(f32))
            at += width
        return outs

    def gather_tokens(side, rows):
        return in_order(side, rows, partner(rows), 1)

    def own_sum(side, partial, seq_count, span_len):
        cut = partial.reshape(seq_count, 2, span_len, -1)
        own = pick(side, cut, 1)
        other = partner(pick(1 - side, cut, 1).astype(bf16))
        return (own + other.astype(f32)).reshape(seq_count * span_len, -1)

    def per_device(
        tokens,
        segments,
        attn_gain,
        query_weight,
        key_weight,
        value_weight,
        output_weight,
        query_gain,
        key_gain,
        ffn_gain,
        gate_weight,
        up_weight,
        down_weight,
        cotangent,
    ):
        side = lax.axis_index("ctx")
        shard_count = lax.axis_size("fsdp") * lax.axis_size("ctx")
        shard_at = lax.axis_index("fsdp") * lax.axis_size("ctx") + side
        seq_count, span_len, width = tokens.shape
        seq_len = segments.shape[1]
        own_count = seq_count * span_len
        tok_count = seq_count * seq_len
        gain_parts = (attn_gain, query_gain, key_gain, ffn_gain)
        gain_sizes = [g.shape[0] for g in gain_parts]
        packed = lax.all_gather(jnp.concatenate(gain_parts)[None], ("fsdp", "ctx"), axis=0, tiled=True)
        gains = []
        at = 0
        for size in gain_sizes:
            gains.append(packed[:, at : at + size].reshape(-1).astype(f32))
            at += size
        gain_one, gain_query, gain_key, gain_two = gains
        head_dim = gain_query.shape[0]
        head_count = query_weight.shape[1] // head_dim
        kv_count = key_weight.shape[1] // head_dim
        group = head_count // kv_count
        half_q = head_count * head_dim // 2
        half_k = kv_count * head_dim // 2
        feed_block = down_weight.shape[0]
        half_ff = gate_weight.shape[1] // 2
        attn_blocks = (group * head_dim, head_dim, head_dim)
        attn_widths = (half_q, half_k, half_k)

        weight_qkv = gather_columns(side, (query_weight, key_weight, value_weight), attn_blocks)
        out_rows = output_weight.shape[0]
        whole_heads = out_rows == group * head_dim
        if whole_heads:
            weight_out = lax.all_gather(output_weight, "fsdp", axis=0, tiled=True)
        else:
            full = lax.all_gather(output_weight, ("fsdp", "ctx"), axis=0, tiled=True)
            full = full.reshape(-1, 2, group * head_dim, width)
            weight_out = pick(side, full, 1).reshape(half_q, width)

        input_rows = tokens.astype(f32).reshape(own_count, width)
        factor_one = rms_scale(input_rows)
        normed_one = input_rows * factor_one
        hidden_own = (normed_one * gain_one).astype(bf16)
        hidden_in = gather_tokens(side, hidden_own.reshape(seq_count, span_len, width)).reshape(
            tok_count, width
        )
        cot_own = cotangent.reshape(own_count, width)
        cot_all = jnp.concatenate([cot_own, partner(cot_own)], axis=0)

        zeros_len = jnp.sum((segments == 0).astype(jnp.int32), axis=1, keepdims=True)
        ones_len = jnp.sum((segments == 1).astype(jnp.int32), axis=1, keepdims=True)
        starts = jnp.where(segments == 0, 0, jnp.where(segments == 1, zeros_len, zeros_len + ones_len))
        positions = (jnp.arange(seq_len, dtype=jnp.int32)[None, :] - starts).astype(f32)
        freq = jnp.power(f32(rope_base), -jnp.arange(head_dim // 2, dtype=f32) * 2.0 / head_dim)
        angle = positions.reshape(tok_count, 1) * freq
        cosine = jnp.cos(angle)
        sine = jnp.sin(angle)
        cos_two = jnp.concatenate([cosine, cosine], axis=-1)
        sin_two = jnp.concatenate([-sine, sine], axis=-1)

        def spread(table, count):
            return jnp.concatenate([table] * count, axis=1)

        def turn(values):
            half = head_dim // 2
            up = jnp.concatenate([values[:, half:], values[:, :half]], axis=1)
            down = jnp.concatenate([values[:, -half:], values[:, :-half]], axis=1)
            lane = jnp.arange(values.shape[1]) % head_dim
            return jnp.where(lane < half, up, down)

        def head_mean(values):
            count = values.shape[1] // head_dim
            ids = jnp.arange(values.shape[1]) // head_dim
            member = (ids[:, None] == jnp.arange(count)[None, :]).astype(f32)
            sums = jnp.dot(values, member, precision=lax.Precision.HIGHEST) / head_dim
            return jnp.dot(sums, member.T, precision=lax.Precision.HIGHEST)

        def head_norm(values):
            factor = lax.rsqrt(head_mean(values * values) + epsilon)
            return factor, values * factor

        qkv = dot_nn(hidden_in, weight_qkv)
        value_low = qkv[:, half_q + half_k :].astype(bf16)
        heads_pre = qkv[:, : half_q + half_k]
        both_count = (half_q + half_k) // head_dim
        gain_both = jnp.concatenate(
            [gain_query] * (half_q // head_dim) + [gain_key] * (half_k // head_dim)
        )
        cos_both = spread(cos_two, both_count)
        sin_both = spread(sin_two, both_count)
        factor_both, normed_both = head_norm(heads_pre)
        scaled_both = normed_both * gain_both
        rotated = (scaled_both * cos_both + turn(scaled_both) * sin_both).astype(bf16)
        query_low = rotated[:, :half_q]
        key_low = rotated[:, half_q:]
        mixed_low, logs = attend(query_low, key_low, value_low, segments, head_dim, group)

        branch = own_sum(side, dot_nn(mixed_low, weight_out), seq_count, span_len)
        resid = input_rows + branch
        factor_two = rms_scale(resid)
        normed_two = resid * factor_two
        second_own = (normed_two * gain_two).astype(bf16)
        second = jnp.concatenate([second_own, partner(second_own)], axis=0)

        weight_gu = gather_columns(side, (gate_weight, up_weight), (feed_block, feed_block))
        weight_down = lax.all_gather(down_weight, "fsdp", axis=0, tiled=True)
        gate_up = dot_nn(second, weight_gu).astype(bf16)
        gate = gate_up[:, :half_ff].astype(f32)
        up = gate_up[:, half_ff:].astype(f32)
        sigma = jax.nn.sigmoid(gate)
        silu = gate * sigma
        act = (silu * up).astype(bf16)
        feed = dot_nn(act, weight_down)
        feed_own = feed[:own_count] + partner(feed[own_count:].astype(bf16)).astype(f32)
        output = (resid + feed_own).astype(bf16).reshape(seq_count, span_len, width)

        grad_down = dot_tn(act, cot_all).astype(bf16)
        down_sum = lax.psum(scatter_rows(grad_down), "replica")
        grad_act = dot_nt(cot_all, weight_down)
        grad_gate = (grad_act * up * (sigma * (1.0 + gate * (1.0 - sigma)))).astype(bf16)
        grad_up = (grad_act * silu).astype(bf16)
        grad_gu = jnp.concatenate([grad_gate, grad_up], axis=1)
        two_part = dot_nt(grad_gu, weight_gu)
        grad_two = two_part[:own_count] + partner(two_part[own_count:].astype(bf16)).astype(f32)
        gu_shard, down_sum = total_after(
            scatter_rows(dot_tn(second, grad_gu).astype(bf16)), down_sum
        )
        grad_gain_two = jnp.sum(grad_two * normed_two, axis=0)
        grad_resid = cot_own.astype(f32) + norm_back(grad_two * gain_two, normed_two, factor_two)

        branch_own = grad_resid.astype(bf16).reshape(seq_count, span_len, width)
        grad_branch = gather_tokens(side, branch_own).reshape(tok_count, width)
        grad_mixed = dot_nt(grad_branch, weight_out).astype(bf16)
        grad_out = dot_tn(mixed_low, grad_branch)
        if whole_heads:
            out_shard = scatter_rows(grad_out.astype(bf16))
        else:
            blocks = grad_out.reshape(-1, 1, group * head_dim, width)
            full = in_order(side, blocks, jnp.zeros_like(blocks), 1).reshape(2 * half_q, width)
            full = lax.psum_scatter(full, ("fsdp", "ctx"), scatter_dimension=0, tiled=True)
            out_shard = full.astype(bf16)
        grad_query, grad_key, grad_value = attend_back(
            query_low, key_low, value_low, segments, mixed_low, grad_mixed, logs, head_dim, group
        )
        grad_both = jnp.concatenate([grad_query, grad_key], axis=1).astype(f32)
        grad_normed = grad_both * cos_both - turn(grad_both) * sin_both
        gain_sums = jnp.sum(grad_normed * normed_both, axis=0).reshape(both_count, head_dim)
        grad_gain_query = jnp.sum(gain_sums[: half_q // head_dim], axis=0)
        grad_gain_key = jnp.sum(gain_sums[half_q // head_dim :], axis=0)
        scaled_grad = grad_normed * gain_both
        pre_both = factor_both * (scaled_grad - normed_both * head_mean(scaled_grad * normed_both))
        grad_qkv = jnp.concatenate([pre_both.astype(bf16), grad_value], axis=1)
        qkv_part = scatter_rows(dot_tn(hidden_in, grad_qkv).astype(bf16))
        (qkv_shard, out_sum), gu_shard = total_after((qkv_part, out_shard), gu_shard)
        out_total = out_sum.astype(f32)
        down_total = down_sum.astype(f32)
        gate_total, up_total = restore_columns(
            side, gu_shard, (half_ff, half_ff), (feed_block, feed_block)
        )
        query_total, key_total, value_total = restore_columns(
            side, qkv_shard, attn_widths, attn_blocks
        )
        grad_one = own_sum(side, dot_nt(grad_qkv, weight_qkv), seq_count, span_len)
        grad_gain_one = jnp.sum(grad_one * normed_one, axis=0)
        input_grad = grad_resid + norm_back(grad_one * gain_one, normed_one, factor_one)

        gain_grads = (grad_gain_one, grad_gain_query, grad_gain_key, grad_gain_two)
        gain_pack = jnp.concatenate(
            [g.reshape(shard_count, -1) for g in gain_grads], axis=1
        )
        gain_pack = pick(shard_at, lax.psum(gain_pack, ("replica", "fsdp", "ctx")), 0)
        gain_totals = []
        at = 0
        for size in gain_sizes:
            gain_totals.append(gain_pack[at : at + size])
            at += size
        return (
            output,
            input_grad.reshape(seq_count, span_len, width),
            gain_totals[0],
            query_total,
            key_total,
            value_total,
            out_total,
            gain_totals[1],
            gain_totals[2],
            gain_totals[3],
            gate_total,
            up_total,
            down_total,
        )

    return per_device


def solution(mesh):
    in_specs = (
        P(("replica", "fsdp"), "ctx", None),
        P(("replica", "fsdp"), None),
        P(("fsdp", "ctx")),
        P(("fsdp", "ctx"), None),
        P(("fsdp", "ctx"), None),
        P(("fsdp", "ctx"), None),
        P(("fsdp", "ctx"), None),
        P(("fsdp", "ctx")),
        P(("fsdp", "ctx")),
        P(("fsdp", "ctx")),
        P(("fsdp", "ctx"), None),
        P(("fsdp", "ctx"), None),
        P(("fsdp", "ctx"), None),
        P(("replica", "fsdp"), "ctx", None),
    )
    out_specs = (
        P(("replica", "fsdp"), "ctx", None),
        P(("replica", "fsdp"), "ctx", None),
        P(("fsdp", "ctx")),
        P(("fsdp", "ctx"), None),
        P(("fsdp", "ctx"), None),
        P(("fsdp", "ctx"), None),
        P(("fsdp", "ctx"), None),
        P(("fsdp", "ctx")),
        P(("fsdp", "ctx")),
        P(("fsdp", "ctx")),
        P(("fsdp", "ctx"), None),
        P(("fsdp", "ctx"), None),
        P(("fsdp", "ctx"), None),
    )
    return jax.shard_map(
        make_per_device(), mesh=mesh, in_specs=in_specs, out_specs=out_specs, check_vma=False
    )
```

time: 1370 us -> 793 us (0.58)
  waiting for transfers between devices: 672 us -> 288 us
  matrix products: 392 us -> 190 us
  Pallas kernels: 0 us -> 58.4 us
  other arithmetic: 113 us -> 77.9 us
    reduce_scatter x9 -> x4, waiting for transfers between devices: 492 us -> 83.9 us  [scatter_rows(): return lax.psum_scatter(grad, 'fsdp', scatter_dimension=0, tiled=True)]
    dot_general x77 -> x16, matrix products: 392 us -> 190 us  [the longest x4 62.1 us: dot_nt(): lax.dot_general(left, right, (((1,), (1,)), ((), ())), preferred_element_...]
    pallas_call x0 -> x2, Pallas kernels: none -> 58.4 us  [the longest x1 41.3 us: attend_back(): pl.pallas_call(body, grid=(seq_count, steps), in_specs=[wide, narrow, nar...]
    psum x1 -> x3, waiting for transfers between devices: 87.3 us -> 136 us  [the longest x2 136 us: total_after(): return (lax.psum(shard, 'replica'), earlier)]
    all_gather x9 -> x4, waiting for transfers between devices: 86.7 us -> 49.8 us  [the longest x1 33.1 us: per_device(): weight_down = lax.all_gather(down_weight, 'fsdp', axis=0, tiled=True)]
    reshape x10 -> x2, local copies, waits for them, and re-layouts: 36.2 us -> 0.16 us  [per_device(): g.reshape(shard_count, -1)]
    convert_element_type x37 -> x13, other arithmetic: 56.7 us -> 24.4 us  [the longest x1 11.9 us: per_device(): (scaled_both * cos_both + turn(scaled_both) * sin_both).astype(bf16)]
    slice x0 -> x16, local copies, waits for them, and re-layouts: none -> 30 us  [the longest x2 13.2 us: turn(): up = jnp.concatenate([values[:, half:], values[:, :half]], axis=1)]
  transfers between devices with their start and end apart: 19 -> 23, of which waited for: 12 -> 13; matrix products, arithmetic and copies ran while one was open for 25% -> 37% of each run, Pallas kernels for 0% -> 7%
where the time goes in v1:
time: 793 us; the launch traced here: 786 us
  waiting for transfers between devices  288 us (36%)
  matrix products  190 us (24%)
  local copies, waits for them, and re-layouts  95.6 us (12%)
  other arithmetic  77.9 us (10%)
  Pallas kernels  58.4 us (7%)
  blocking collectives  55.9 us (7%)
  between operations  16.1 us (2%)
    psum x2, waiting for transfers between devices, total_after(): return (lax.psum(shard, 'replica'), earlier)  136 us
    reduce_scatter x4, waiting for transfers between devices, scatter_rows(): return lax.psum_scatter(grad, 'fsdp', scatter_dimension=0, tiled=True)  83.9 us
    dot_general x4, matrix products, dot_nt(): lax.dot_general(left, right, (((1,), (1,)), ((), ())), preferred_element_...  62.1 us
    dot_general x4, matrix products, dot_nn(): return jnp.dot(left, right, preferred_element_type=f32)  51 us
    dot_general x4, matrix products, dot_tn(): lax.dot_general(left, right, (((0,), (0,)), ((), ())), preferred_element_...  50.4 us
    pallas_call x1, Pallas kernels, attend_back(): pl.pallas_call(body, grid=(seq_count, steps), in_specs=[wide, narrow, nar...  41.3 us
    psum x1, blocking collectives, per_device(): lax.psum(gain_pack, ('replica', 'fsdp', 'ctx'))  40 us
    unnamed x133, local copies, waits for them, and re-layouts  33.7 us
  transfers between devices with their start and end apart: 23, of which 13 were waited for; matrix products, arithmetic and copies ran while one was open for 37% of the time, Pallas kernels for 7%

profile of v1, /device:TPU:0, one launch (start us, length us, event | category | flops | bytes accessed | tf_op | source)
XLA Modules:
  0.0 786.1 jit_solution(13530780857610810804)
XLA Ops:
  21.9 15.9 %all-reduce = bf16[2176]{0:T(1024)(128)(2,1)S(1)} all-reduce(bf16[2176]{0:T(1024)(128)(2,1)S(1)} %dynamic-update-slice), channel_id=2, replica_groups=mesh['replica'=4,'fsdp'=4,'ctx'=2] {'fsdp','ctx'}, use_global_device_ids=true, to_apply=%add | all-reduce | flops 2176 | bytes 8704
  45.4 10.8 %concatenate.95 = f32[2048,768]{1,0:T(8,128)} concatenate(f32[2048,32]{1,0:T(8,128)S(1)} %get-tuple-element.148, f32[2048,32]{1,0:T(8,128)S(1)} %get-tuple-element.148, f32[2048,32]{1,0:T(8,128)S(1)} %get-tuple-element.148, f32[2048,32]{1,0:T(8,128)S(1)} %get-tuple-element.148, f32[2048,32]{1,0:T(8,128)S(1)} %get-tuple-element.148, f32[2048,32]{1,0:T(8,128)S(1)} %get-tuple-element.148, ...), dimensions={1} | concatenate | bytes 12582912 | tf_op jit(solution)/shard_map/concatenate | solution.py:331
  56.6 10.5 %concatenate.98 = f32[2048,768]{1,0:T(8,128)} concatenate(f32[2048,32]{1,0:T(8,128)S(1)} %get-tuple-element.149, f32[2048,32]{1,0:T(8,128)S(1)} %get-tuple-element.150, f32[2048,32]{1,0:T(8,128)S(1)} %get-tuple-element.149, f32[2048,32]{1,0:T(8,128)S(1)} %get-tuple-element.150, f32[2048,32]{1,0:T(8,128)S(1)} %get-tuple-element.149, f32[2048,32]{1,0:T(8,128)S(1)} %get-tuple-element.150, ...), dimensions={1} | concatenate | bytes 12582912 | tf_op jit(solution)/shard_map/concatenate | solution.py:331
  92.2 11.5 %fusion.80 = (f32[2048,736]{1,0:T(8,128)}, f32[2048,736]{1,0:T(8,128)}) fusion(f32[2048,768]{1,0:T(8,128)} %copy-done.20), kind=kLoop, calls=%fused_computation.187 | loop fusion | bytes 24117248 | tf_op jit(solution)/shard_map/slice | solution.py:336
  103.7 11.9 %fusion.13 = bf16[2048,768]{1,0:T(8,128)(2,1)S(1)} fusion(f32[2048,768]{1,0:T(8,128)} %concatenate.98, f32[2048,32]{1,0:T(8,128)S(1)} %get-tuple-element.109, f32[2048,736]{1,0:T(8,128)} %get-tuple-element.111, f32[2048,736]{1,0:T(8,128)} %get-tuple-element.110, f32[2048,32]{1,0:T(8,128)S(1)} %get-tuple-element.108, f32[2048,768]{1,0:T(8,128)} %copy-done.20, ...), kind=kLoop, calls=%fused_computation.22 | loop fusion | flops 11010048 | bytes 34603776 | tf_op jit(solution)/shard_map/convert_element_type | solution.py:362
  118.7 17.2 %shard_map.237 = (bf16[2048,512]{1,0:T(8,128)(2,1)S(1)}, f32[4,1024,4]{2,1,0:T(8,128)S(1)}) custom-call(bf16[2048,512]{1,0:T(8,128)(2,1)S(1)} %slice.249.refs_0_, bf16[2048,256]{1,0:T(8,128)(2,1)S(1)} %slice.250.refs_1_, bf16[2048,256]{1,0:T(8,128)(2,1)S(1)} %slice.364.refs_2_, s32[2,1024,1]{2,1,0:T(8,128)S(1)} %copy.118.refs_3_, ...), custom_call_target="tpu_custom_call" | custom-call | flops 4294967296 | bytes 8388608 | tf_op jit(solution)/shard_map/pallas_call | solution.py:149
  161.9 16.7 %all-gather.10.cloned.1.call-done = bf16[1024,4608]{0,1:T(8,128)(2,1)} async-done(((bf16[256,4608]{0,1:T(8,128)(2,1)}), bf16[1024,4608]{0,1:T(8,128)(2,1)}) %all-gather.10.cloned.1.call-update) | async-done | bytes 9437200 | tf_op jit(solution)/shard_map/all_gather | solution.py:225
  178.6 25.7 %convolution_convert_fusion = bf16[2048,4608]{1,0:T(8,128)(2,1)} fusion(bf16[1024,4608]{0,1:T(8,128)(2,1)} %all-gather.10.cloned.1.call-done, bf16[1024,1024]{1,0:T(8,128)(2,1)S(1)} %collective-permute-done.3, bf16[1024,1024]{1,0:T(8,128)(2,1)} %copy-done.29), kind=kOutput, calls=%fused_computation.5 | convolution fusion | flops 19345178624 | bytes 32505856 | tf_op jit(solution)/shard_map/dot_general | solution.py:33
  204.3 33.1 %all-gather.12.cloned.1.call-done = bf16[2304,1024]{1,0:T(8,128)(2,1)} async-done(((bf16[576,1024]{1,0:T(8,128)(2,1)}), bf16[2304,1024]{1,0:T(8,128)(2,1)}) %all-gather.12.cloned.1.call-update) | async-done | bytes 4718608 | tf_op jit(solution)/shard_map/all_gather | solution.py:375
  237.4 27.1 %fusion.2 = (bf16[2048,2304]{1,0:T(8,128)(2,1)}, bf16[2048,2304]{1,0:T(8,128)(2,1)}, bf16[2048,2304]{1,0:T(8,128)(2,1)}) fusion(bf16[2048,4608]{1,0:T(8,128)(2,1)} %convolution_convert_fusion, bf16[2304,1024]{1,0:T(8,128)(2,1)} %all-gather.12.cloned.1.call-done, bf16[1024,1024]{1,0:T(8,128)(2,1)} %collective-permute-done.6, bf16[1024,1024]{1,0:T(8,128)(2,1)} %bitcast.26), kind=kOutput, calls=%fused_computation.8 | convolution fusion | flops 9752281088 | bytes 56098816 | tf_op jit(solution)/shard_map/dot_general | solution.py:25
  264.5 15.5 %convolution_convert_fusion.1 = bf16[2304,1024]{1,0:T(8,128)(2,1)} fusion(bf16[2048,2304]{1,0:T(8,128)(2,1)} %get-tuple-element.102, bf16[1024,1024]{1,0:T(8,128)(2,1)} %collective-permute-done.6, bf16[1024,1024]{1,0:T(8,128)(2,1)} %bitcast.26), kind=kOutput, calls=%fused_computation.36 | convolution fusion | flops 9674424320 | bytes 18350080 | tf_op jit(solution)/shard_map/dot_general | solution.py:29
  280.1 57.2 %reduce-scatter.11.cloned.1.call-done = bf16[576,1024]{1,0:T(8,128)(2,1)} async-done(((bf16[2304,1024]{1,0:T(8,128)(2,1)}), bf16[576,1024]{1,0:T(8,128)(2,1)}) %reduce-scatter.11.cloned.1.call-update) | async-done | bytes 1179664 | tf_op jit(solution)/shard_map/reduce_scatter | solution.py:228
  337.4 25.8 %fusion.10 = bf16[1024,4608]{1,0:T(8,128)(2,1)} fusion(bf16[2048,2304]{1,0:T(8,128)(2,1)} %get-tuple-element.101, bf16[2048,2304]{1,0:T(8,128)(2,1)} %get-tuple-element.100, bf16[1024,1024]{1,0:T(8,128)(2,1)} %copy-done.55, bf16[1024,1024]{1,0:T(8,128)(2,1)S(1)} %copy-done.30), kind=kOutput, calls=%fused_computation.18 | convolution fusion | flops 19378208768 | bytes 32505856 | tf_op jit(solution)/shard_map/dot_general | solution.py:29
  363.2 25.8 %fusion.9 = f32[2048,1024]{1,0:T(8,128)S(1)} fusion(bf16[1024,4608]{0,1:T(8,128)(2,1)} %all-gather.10.cloned.1.call-done, bf16[2048,2304]{1,0:T(8,128)(2,1)} %get-tuple-element.101, bf16[2048,2304]{1,0:T(8,128)(2,1)} %get-tuple-element.100), kind=kOutput, calls=%fused_computation.17 | convolution fusion | flops 19365101568 | bytes 36700160 | tf_op jit(solution)/shard_map/dot_general | solution.py:25
  389.4 14.0 %fusion.84 = f32[2048,1024]{1,0:T(8,128)S(1)} fusion(bf16[2048,2304]{1,0:T(8,128)(2,1)} %get-tuple-element.102, bf16[2304,1024]{1,0:T(8,128)(2,1)} %all-gather.12.cloned.1.call-done), kind=kOutput, calls=%fused_computation.191 | convolution fusion | flops 9663676416 | bytes 22544384 | tf_op jit(solution)/shard_map/dot_general | solution.py:33
  423.0 41.3 %shard_map.238 = (bf16[2048,512]{1,0:T(8,128)(2,1)S(1)}, bf16[2048,256]{1,0:T(8,128)(2,1)S(1)}, bf16[2048,256]{1,0:T(8,128)(2,1)S(1)}) custom-call(bf16[2048,512]{1,0:T(8,128)(2,1)S(1)} %copy-done.1, bf16[2048,256]{1,0:T(8,128)(2,1)S(1)} %copy-done.5, bf16[2048,256]{1,0:T(8,128)(2,1)S(1)} %copy-done.7, s32[2,1024,1]{2,1,0:T(8,128)S(1)} %copy-done.3, ...), custom_call_target="tpu_custom_call" | custom-call | flops 10737418240 | bytes 16777216 | tf_op jit(solution)/shard_map/pallas_call | solution.py:178
  471.9 11.3 %fusion.77 = (f32[2048,736]{1,0:T(8,128)}, f32[2048,736]{1,0:T(8,128)}) fusion(f32[2048,768]{1,0:T(8,128)} %copy-done.21), kind=kLoop, calls=%fused_computation.184 | loop fusion | bytes 24117248 | tf_op jit(solution)/shard_map/slice | solution.py:335
  483.3 17.0 %multiply_reduce_fusion = (f32[768]{0:T(1024)S(1)}, f32[2048,768]{1,0:T(8,128)}) fusion(f32[2048,768]{1,0:T(8,128)} %get-tuple-element.158, f32[2048,1024]{1,0:T(8,128)} %copy-done.19, f32[2048,768]{1,0:T(8,128)} %concatenate.98, f32[2048,736]{1,0:T(8,128)} %get-tuple-element.104, f32[2048,32]{1,0:T(8,128)} %get-tuple-element.106, ...), kind=kLoop, calls=%fused_computation.26 | loop fusion | flops 22019328 | bytes 47189760 | tf_op jit(solution)/shard_map/reduce_sum | solution.py:416
  500.3 8.6 %fusion.44 = f32[2048,12]{0,1:T(8,128)S(1)} fusion(f32[2048,768]{1,0:T(8,128)} %get-tuple-element.94, f32[768]{0:T(1024)S(1)} %copy-done.46, s32[768]{0:T(1024)S(1)} %copy-done.38, f32[2048,1024]{1,0:T(8,128)} %copy-done.19, f32[2048,768]{1,0:T(8,128)} %get-tuple-element.158), kind=kOutput, calls=%fused_computation.84 | convolution fusion | flops 232817664 | bytes 18978816 | tf_op jit(solution)/shard_map/dot_general | solution.py:344
  509.1 9.5 %multiply_convert_fusion.1 = bf16[2048,768]{1,0:T(8,128)(2,1)S(1)} fusion(f32[2048,768]{1,0:T(8,128)} %get-tuple-element.94, f32[2048,768]{1,0:T(8,128)} %get-tuple-element.158, f32[2048,12]{0,1:T(8,128)S(1)} %fusion.44, f32[768]{0:T(1024)S(1)} %copy-done.46, s32[768]{0:T(1024)S(1)} %copy-done.38, f32[2048,1024]{1,0:T(8,128)} %copy-done.19), kind=kOutput, calls=%fused_computation.27 | convolution fusion | flops 237511680 | bytes 22124544 | tf_op jit(solution)/shard_map/dot_general | solution.py:345
  549.2 26.7 %reduce-scatter.5.cloned.1.call-done = bf16[256,1024]{1,0:T(8,128)(2,1)} async-done(((bf16[1024,1024]{1,0:T(8,128)(2,1)}), bf16[256,1024]{1,0:T(8,128)(2,1)}) %reduce-scatter.5.cloned.1.call-update) | async-done | bytes 524304 | tf_op jit(solution)/shard_map/reduce_scatter | solution.py:228
  575.9 97.9 %all-reduce.8.cloned.1.call-done = bf16[256,4608]{1,0:T(8,128)(2,1)} async-done(((bf16[256,4608]{1,0:T(8,128)(2,1)}), bf16[256,4608]{1,0:T(8,128)(2,1)}) %all-reduce.8.cloned.1.call-update) | async-done | bytes 2359312 | tf_op jit(solution)/shard_map/psum | solution.py:232
  681.2 38.0 %all-reduce.10.cloned.1.call-done = (bf16[2,128,1024]{2,1,0:T(8,128)(2,1)}, bf16[128,1024]{1,0:T(8,128)(2,1)}) async-done(((bf16[2,128,1024]{2,1,0:T(8,128)(2,1)}, bf16[128,1024]{1,0:T(8,128)(2,1)}), (bf16[2,128,1024]{2,1,0:T(8,128)(2,1)}, bf16[128,1024]{1,0:T(8,128)(2,1)})) %all-reduce.10.cloned.1.call-update) | async-done | bytes 786448 | tf_op jit(solution)/shard_map/psum | solution.py:232
  721.8 40.0 %psum.35 = f32[8,272]{1,0:T(8,128)S(1)} all-reduce(f32[8,272]{1,0:T(8,128)S(1)} %pad_maximum_fusion.24), channel_id=1, replica_groups=mesh['replica'=4,'fsdp'=4,'ctx'=2] {'replica','fsdp','ctx'}, use_global_device_ids=true, to_apply=%region_11.12 | all-reduce | flops 2176 | bytes 17408 | tf_op jit(solution)/shard_map/psum | solution.py:440
  (276 shorter events, 161.0 us)
Async XLA Ops:
  7.2 65.7 %all-gather.6.cloned.1.call-start = ((), (), s32[]{:S(2)}) async-start(), calls=%async_computation.4 | async-start | bytes 2621440 | tf_op jit(solution)/shard_map/all_gather | solution.py:225
  10.7 1.7 collective-permute-start.1
  13.3 124.8 %all-gather.8.cloned.1.call-start = ((), (), s32[]{:S(2)}) async-start(), calls=%async_computation.5 | async-start | bytes 1310720 | tf_op jit(solution)/shard_map/all_gather | solution.py:303
  15.1 2.9 collective-permute-start.4
  15.6 163.0 %all-gather.10.cloned.1.call-start = ((), (), s32[]{:S(2)}) async-start(), calls=%async_computation.6 | async-start | bytes 11796480 | tf_op jit(solution)/shard_map/all_gather | solution.py:225
  20.3 217.1 %all-gather.12.cloned.1.call-start = ((), (), s32[]{:S(2)}) async-start(), calls=%async_computation.7 | async-start | bytes 5898240 | tf_op jit(solution)/shard_map/all_gather | solution.py:375
  39.1 116.7 %copy-start.41 = (f32[1024]{0:T(1024)}, f32[1024]{0:T(1024)S(1)}, u32[]{:S(2)}) copy-start(f32[1024]{0:T(1024)S(1)} %get-tuple-element.152) | copy-start | bytes 12292
  41.0 26.1 %collective-permute-start = (bf16[2,512,1024]{2,1,0:T(8,128)(2,1)}, bf16[2,512,1024]{2,1,0:T(8,128)(2,1)}, u32[]{:S(2)}, u32[]{:S(2)}) collective-permute-start(bf16[2,512,1024]{2,1,0:T(8,128)(2,1)} %fusion.30), channel_id=1, source_target_pairs={{0,1},{1,0},{2,3},{3,2},{4,5},{5,4},{6,7},{7,6},{8,9},{9,8},{10,11... | collective-permute-start | bytes 6291464 | tf_op jit(solution)/shard_map/ppermute | solution.py:203
  147.5 4.6 collective-permute-start.2
  148.0 189.3 %reduce-scatter.11.cloned.1.call-start = ((), (), s32[]{:S(2)}) async-start(), calls=%async_computation.11 | async-start | bytes 5898240 | tf_op jit(solution)/shard_map/reduce_scatter | solution.py:228
  157.8 4.2 collective-permute-start.3
  159.1 45.2 %collective-permute-start.6 = (bf16[1024,1024]{1,0:T(8,128)(2,1)}, bf16[1024,1024]{1,0:T(8,128)(2,1)}, u32[]{:S(2)}, u32[]{:S(2)}) collective-permute-start(bf16[1024,1024]{1,0:T(8,128)(2,1)} %bitcast.26), channel_id=1, source_target_pairs={{0,1},{1,0},{2,3},{3,2},{4,5},{5,4},{6,7},{7,6},{8,9},{9,8},{10,11... | collective-permute-start | bytes 6291464 | tf_op jit(solution)/shard_map/ppermute | solution.py:203
  280.0 258.6 %all-reduce.6.cloned.1.call-start = ((), (), s32[]{:S(2)}) async-start(), calls=%async_computation.12 | async-start | bytes 2359296 | tf_op jit(solution)/shard_map/psum | solution.py:387
  337.3 201.3 %reduce-scatter.9.cloned.1.call-start = ((), (), s32[]{:S(2)}) async-start(), calls=%async_computation.10 | async-start | bytes 11796480 | tf_op jit(solution)/shard_map/reduce_scatter | solution.py:228
  363.2 186.0 %reduce-scatter.7.cloned.1.call-start = ((), (), s32[]{:S(2)}) async-start(), calls=%async_computation.9 | async-start | bytes 1310720 | tf_op jit(solution)/shard_map/reduce_scatter | solution.py:228
  389.4 15.0 %collective-permute-start.7 = (bf16[1024,1024]{1,0:T(8,128)(2,1)S(1)}, bf16[1024,1024]{1,0:T(8,128)(2,1)S(1)}, u32[]{:S(2)}, u32[]{:S(2)}) collective-permute-start(bf16[1024,1024]{1,0:T(8,128)(2,1)S(1)} %slice.362), channel_id=1, source_target_pairs={{0,1},{1,0},{2,3},{3,2},{4,5},{5,4},{6,7},{7,6},{8,9},{9,8},{10,11... | collective-permute-start | bytes 6291464 | tf_op jit(solution)/shard_map/ppermute | solution.py:203
  403.8 4.5 collective-permute-start.5
  413.9 4.2 collective-permute-start.8
  509.0 66.9 %reduce-scatter.5.cloned.1.call-start = ((), (), s32[]{:S(2)}) async-start(), calls=%async_computation.8 | async-start | bytes 2621440 | tf_op jit(solution)/shard_map/reduce_scatter | solution.py:228
  526.2 147.5 %all-reduce.8.cloned.1.call-start = ((), (), s32[]{:S(2)}) async-start(), calls=%async_computation.13 | async-start | bytes 4718592 | tf_op jit(solution)/shard_map/psum | solution.py:232
  538.3 4.5 collective-permute-start.9
  538.7 180.5 %all-reduce.10.cloned.1.call-start = ((), (), s32[]{:S(2)}) async-start(), calls=%async_computation.14 | async-start | bytes 1572864 | tf_op jit(solution)/shard_map/psum | solution.py:232
  681.2 91.9 %collective-permute-start.11 = (bf16[128,4608]{0,1:T(8,128)(2,1)}, bf16[128,4608]{0,1:T(8,128)(2,1)}, u32[]{:S(2)}, u32[]{:S(2)}) collective-permute-start(bf16[128,4608]{0,1:T(8,128)(2,1)} %bitcast.184), channel_id=1, source_target_pairs={{0,1},{1,0},{2,3},{3,2},{4,5},{5,4},{6,7},{7,6},{8,9},{9,8},{10,11... | collective-permute-start | bytes 3538952 | tf_op jit(solution)/shard_map/ppermute | solution.py:203
  721.7 46.6 %collective-permute-start.10 = (bf16[128,1024]{0,1:T(8,128)(2,1)}, bf16[128,1024]{0,1:T(8,128)(2,1)}, u32[]{:S(2)}, u32[]{:S(2)}) collective-permute-start(bf16[128,1024]{0,1:T(8,128)(2,1)} %bitcast.40), channel_id=1, source_target_pairs={{0,1},{1,0},{2,3},{3,2},{4,5},{5,4},{6,7},{7,6},{8,9},{9,8},{10,11... | collective-permute-start | bytes 786440 | tf_op jit(solution)/shard_map/ppermute | solution.py:203
  (57 other events, 742.7 us)
Sparse Core Ops, SparseCore 0:
  13.5 37.9 all-gather.5
  53.3 26.6 all-gather.7
  82.4 96.1 all-gather.9
  180.3 57.0 all-gather.11
  280.2 57.0 reduce-scatter.10
  339.5 55.8 all-reduce.5
  398.6 94.5 reduce-scatter.8
  509.1 27.6 reduce-scatter.6
  540.7 35.1 reduce-scatter.4
  578.1 95.6 all-reduce.7
  676.2 42.9 all-reduce.9
